TPU v7x, 32 devices: a whole 2x2x4 slice. The times are simulated.
32 devices in a mesh: fsdp: 8 (over z, x), seq: 4 (over y, core).
Axes of the slice: x: 2, y: 2, z: 4, core: 2. Of those that a mesh axis runs over, the one named last changes fastest.
Arguments:
- tokens: bfloat16 [8, 512, 768], P('fsdp', 'seq'), may hold values from -6 to 6
- encoder: bfloat16 [8, 512, 768], P('fsdp'), may hold values from -6 to 6
- dec_segments: int32 [8, 512], P('fsdp'), may hold values from 0 to 2, never falling along the last dimension, each value on 1 to 320 neighbouring positions
- enc_segments: int32 [8, 512], P('fsdp'), may hold values from 0 to 2, never falling along the last dimension, each value on 1 to 320 neighbouring positions
- buckets: int32 [512], replicated, may hold values from 0 to 31, as said below
- self_gain: bfloat16 [768], P(('fsdp', 'seq')), may hold values from 0.5 to 1.5
- self_query: bfloat16 [589824], P(('fsdp', 'seq')), may hold values from -0.0546875 to 0.0546875
- self_key: bfloat16 [589824], P(('fsdp', 'seq')), may hold values from -0.21875 to 0.21875
- self_value: bfloat16 [589824], P(('fsdp', 'seq')), may hold values from -0.21875 to 0.21875
- self_output: bfloat16 [589824], P(('fsdp', 'seq')), may hold values from -0.625 to 0.625
- bias_table: bfloat16 [32, 12], replicated, may hold values from -4 to 4
- cross_gain: bfloat16 [768], P(('fsdp', 'seq')), may hold values from 0.5 to 1.5
- cross_query: bfloat16 [589824], P(('fsdp', 'seq')), may hold values from -0.0546875 to 0.0546875
- cross_key: bfloat16 [589824], P(('fsdp', 'seq')), may hold values from -0.21875 to 0.21875
- cross_value: bfloat16 [589824], P(('fsdp', 'seq')), may hold values from -0.21875 to 0.21875
- cross_output: bfloat16 [589824], P(('fsdp', 'seq')), may hold values from -0.625 to 0.625
- ffn_gain: bfloat16 [768], P(('fsdp', 'seq')), may hold values from 0.5 to 1.5
- ffn_gate: bfloat16 [1572864], P(('fsdp', 'seq')), may hold values from -0.21875 to 0.21875
- ffn_up: bfloat16 [1572864], P(('fsdp', 'seq')), may hold values from -0.21875 to 0.21875
- ffn_down: bfloat16 [1572864], P(('fsdp', 'seq')), may hold values from -0.25 to 0.25
- cotangent: bfloat16 [8, 512, 768], P('fsdp', 'seq'), may hold values from -6 to 6
Outputs:
- output: bfloat16 [8, 512, 768], P('fsdp', 'seq')
- grad_tokens: float32 [8, 512, 768], P('fsdp', 'seq')
- grad_encoder: float32 [8, 512, 768], P('fsdp', 'seq')
- grad_self_gain: float32 [768], P(('fsdp', 'seq'))
- grad_self_query: float32 [589824], P(('fsdp', 'seq'))
- grad_self_key: float32 [589824], P(('fsdp', 'seq'))
- grad_self_value: float32 [589824], P(('fsdp', 'seq'))
- grad_self_output: float32 [589824], P(('fsdp', 'seq'))
- grad_bias_table: float32 [32, 12], replicated
- grad_cross_gain: float32 [768], P(('fsdp', 'seq'))
- grad_cross_query: float32 [589824], P(('fsdp', 'seq'))
- grad_cross_key: float32 [589824], P(('fsdp', 'seq'))
- grad_cross_value: float32 [589824], P(('fsdp', 'seq'))
- grad_cross_output: float32 [589824], P(('fsdp', 'seq'))
- grad_ffn_gain: float32 [768], P(('fsdp', 'seq'))
- grad_ffn_gate: float32 [1572864], P(('fsdp', 'seq'))
- grad_ffn_up: float32 [1572864], P(('fsdp', 'seq'))
- grad_ffn_down: float32 [1572864], P(('fsdp', 'seq'))
Inputs may be any that keep to these rules, and one draw needn't show every extreme that they name: buckets[d] is the bucket of a key d positions before its query; it never falls as d grows, equals d for d below 16, and its last entry is 31. `dec_segments`: along each row the ids never fall; every id 0 to 2 appears; the longest document has 320 positions. `enc_segments`: along each row the ids never fall; every id 0 to 2 appears, so each decoder document has encoder positions in its row; the longest has 320 positions.
All inputs are finite; a program needn't handle non-finite values.
Results may differ from a plain program's by a relative error of at most 0.023.
The roundings to bfloat16 on the way count: a program that leaves them out, or rounds other values in their place, can miss the bound.
Values may be sent and summed in bfloat16 or wider, within the bound.
A program may use at most 256 MiB of HBM per device.

v0:
```python
import jax
import jax.numpy as jnp
from jax import lax
from jax.sharding import PartitionSpec as P

HEADS = 12
HEAD_DIM = 64
epsilon = 1e-06
masked_value = -1e30
highest = lax.Precision.HIGHEST


def matmul(first_op, second_op):
    return jnp.dot(first_op, second_op, preferred_element_type=jnp.float32)


def contract_rows(first_op, second_op):
    return lax.dot_general(
        first_op, second_op, (((0,), (0,)), ((), ())), preferred_element_type=jnp.float32
    )


def times_transposed(first_op, second_op):
    return lax.dot_general(
        first_op, second_op, (((1,), (1,)), ((), ())), preferred_element_type=jnp.float32
    )


def rms_forward(values, gain_vector):
    factor = lax.rsqrt(jnp.mean(values * values, axis=-1, keepdims=True) + epsilon)
    return ((values * factor * gain_vector.astype(jnp.float32)).astype(jnp.bfloat16), factor)


def rms_backward(values, factor, gain_vector, upstream):
    scaled = upstream * gain_vector.astype(jnp.float32)
    inner_mean = jnp.mean(scaled * values, axis=-1, keepdims=True)
    grad_values = factor * scaled - values * (factor * factor * factor) * inner_mean
    grad_gain = jnp.sum(upstream * values * factor, axis=0)
    return (grad_values, grad_gain)


def gather_rows(packed):
    return lax.all_gather(packed, ("fsdp", "seq"), axis=0, tiled=True)


def scatter_rows(partial):
    return lax.psum_scatter(partial, ("fsdp", "seq"), scatter_dimension=0, tiled=True)


def scatter_to_owner(partial, row_count, block):
    count = lax.axis_size("seq")
    index = lax.axis_index("seq")
    total = lax.dynamic_slice_in_dim(partial, index * block, block, 1).astype(jnp.float32)
    for step in range(1, count):
        target = lax.rem(index + step, count)
        piece = lax.dynamic_slice_in_dim(partial, target * block, block, 1)
        pairs = [(source, (source + step) % count) for source in range(count)]
        total = total + lax.ppermute(piece, "seq", pairs).astype(jnp.float32)
    return total.astype(jnp.bfloat16)


def sum_everywhere(values):
    for axis in ("seq", "fsdp"):
        count = lax.axis_size(axis)
        step = 1
        while step < count:
            pairs = [(source, source ^ step) for source in range(count)]
            values = values + lax.ppermute(values, axis, pairs)
            step *= 2
    return values


def split_heads(values, row_count):
    return values.reshape(row_count, -1, HEADS, HEAD_DIM)


def score_block(query_heads, key_heads, position_bias, allowed):
    scores = (
        jnp.einsum("rqhd,rkhd->rhqk", query_heads, key_heads, preferred_element_type=jnp.float32)
        + position_bias
    )
    return jnp.where(allowed[:, None], scores, masked_value)


def attend(query_heads, key_heads, value_heads, position_bias, allowed):
    scores = score_block(query_heads, key_heads, position_bias, allowed)
    maximum = jnp.max(scores, axis=-1, keepdims=True)
    log_total = maximum + jnp.log(jnp.sum(jnp.exp(scores - maximum), axis=-1, keepdims=True))
    attn_probs = jnp.exp(scores - log_total).astype(jnp.bfloat16)
    mixed_heads = jnp.einsum(
        "rhqk,rkhd->rqhd", attn_probs, value_heads, preferred_element_type=jnp.float32
    )
    return (mixed_heads.astype(jnp.bfloat16), log_total)


def attend_back(query_heads, key_heads, value_heads, position_bias, allowed, log_total, grad_mixed):
    scores = score_block(query_heads, key_heads, position_bias, allowed)
    attn_probs = jnp.exp(scores - log_total)
    grad_probs = jnp.einsum(
        "rqhd,rkhd->rhqk", grad_mixed, value_heads, preferred_element_type=jnp.float32
    )
    grad_value = jnp.einsum(
        "rhqk,rqhd->rkhd",
        attn_probs.astype(jnp.bfloat16),
        grad_mixed,
        preferred_element_type=jnp.float32,
    )
    row_sums = jnp.sum(attn_probs * grad_probs, axis=-1, keepdims=True)
    grad_scores = attn_probs * (grad_probs - row_sums)
    low_scores = grad_scores.astype(jnp.bfloat16)
    grad_query = jnp.einsum(
        "rhqk,rkhd->rqhd", low_scores, key_heads, preferred_element_type=jnp.float32
    ).astype(jnp.bfloat16)
    grad_key = jnp.einsum(
        "rhqk,rqhd->rkhd", low_scores, query_heads, preferred_element_type=jnp.float32
    )
    return (grad_scores, grad_query, grad_key, grad_value)


def geglu(gate_part, up_part):
    return jax.nn.gelu(gate_part, approximate=True) * up_part


def per_device(
    tokens,
    encoder,
    dec_segments,
    enc_segments,
    buckets,
    self_gain,
    self_query,
    self_key,
    self_value,
    self_output,
    bias_table,
    cross_gain,
    cross_query,
    cross_key,
    cross_value,
    cross_output,
    ffn_gain,
    ffn_gate,
    ffn_up,
    ffn_down,
    cotangent,
):
    row_count, block_len, model_width = tokens.shape
    full_len = dec_segments.shape[1]
    enc_len = encoder.shape[1]
    seq_count = lax.axis_size("seq")
    seq_index = lax.axis_index("seq")
    enc_block = enc_len // seq_count
    inputs_flat = tokens.reshape(row_count * block_len, model_width).astype(jnp.float32)
    query_pos = seq_index * block_len + jnp.arange(block_len, dtype=jnp.int32)
    key_pos = jnp.arange(full_len, dtype=jnp.int32)
    distance = query_pos[:, None] - key_pos[None, :]
    bucket_ids = jnp.arange(bias_table.shape[0], dtype=jnp.int32)
    first = jnp.sum((buckets[None, :] < bucket_ids[:, None]).astype(jnp.int32), axis=1)
    beyond = jnp.sum((buckets[None, :] <= bucket_ids[:, None]).astype(jnp.int32), axis=1)
    clipped = jnp.clip(distance, 0, full_len - 1)[:, None, :]
    onehot = ((clipped >= first[None, :, None]) & (clipped < beyond[None, :, None])).astype(
        jnp.bfloat16
    )
    position_bias = jnp.einsum(
        "qbk,bh->hqk", onehot, bias_table, preferred_element_type=jnp.float32
    )
    own_segments = lax.dynamic_slice_in_dim(dec_segments, seq_index * block_len, block_len, 1)
    self_allowed = (distance >= 0)[None] & (own_segments[:, :, None] == dec_segments[:, None, :])
    cross_allowed = own_segments[:, :, None] == enc_segments[:, None, :]
    own_rows = self_gain.shape[0]
    gains = jnp.pad(jnp.stack([self_gain, cross_gain, ffn_gain], axis=1), ((0, 0), (0, 125)))

    def rows_of(flat):
        return flat.reshape(own_rows, -1)

    packed_self = gather_rows(
        jnp.concatenate(
            [rows_of(w) for w in (self_query, self_key, self_value, self_output)] + [gains], axis=1
        )
    )
    packed_rest = gather_rows(
        jnp.concatenate(
            [
                rows_of(w)
                for w in (cross_query, cross_key, cross_value, cross_output, ffn_gate, ffn_up)
            ],
            axis=1,
        )
    )
    packed_cross = packed_rest[:, : 4 * model_width]
    packed_in = packed_rest[:, 4 * model_width :]
    packed_down = gather_rows(ffn_down.reshape(-1, model_width))
    all_gains = packed_self[:, 4 * model_width :]

    def columns(packed, index):
        return packed[:, index * model_width : (index + 1) * model_width]

    hidden_width = packed_down.shape[0]
    self_full = [all_gains[:, 0]] + [columns(packed_self, index) for index in range(4)]
    cross_full = [all_gains[:, 1]] + [columns(packed_cross, index) for index in range(4)]
    ffn_full = [
        all_gains[:, 2],
        packed_in[:, :hidden_width],
        packed_in[:, hidden_width:],
        packed_down,
    ]
    norm_one, factor_one = rms_forward(inputs_flat, self_full[0])
    qkv_one = matmul(norm_one, packed_self[:, : 3 * model_width]).astype(jnp.bfloat16)
    query_one = qkv_one[:, :model_width]
    pair_all = lax.all_gather(
        qkv_one[:, model_width:].reshape(row_count, block_len, 2 * model_width),
        "seq",
        axis=1,
        tiled=True,
    )
    key_all = pair_all[:, :, :model_width]
    value_all = pair_all[:, :, model_width:]
    query_heads_one = split_heads(query_one, row_count)
    key_heads_one = split_heads(key_all, row_count)
    value_heads_one = split_heads(value_all, row_count)
    mixed_one, lse_one = attend(
        query_heads_one, key_heads_one, value_heads_one, position_bias[None], self_allowed
    )
    mixed_one = mixed_one.reshape(row_count * block_len, model_width)
    hidden_one = inputs_flat + matmul(mixed_one, self_full[4])
    norm_two, factor_two = rms_forward(hidden_one, cross_full[0])
    query_two = matmul(norm_two, cross_full[1]).astype(jnp.bfloat16)
    enc_own = lax.dynamic_slice_in_dim(encoder, seq_index * enc_block, enc_block, 1).reshape(
        row_count * enc_block, model_width
    )
    enc_flat = encoder.reshape(row_count * enc_len, model_width)
    key_two = matmul(enc_flat, cross_full[2]).astype(jnp.bfloat16)
    value_two = matmul(enc_flat, cross_full[3]).astype(jnp.bfloat16)
    query_heads_two = split_heads(query_two, row_count)
    key_heads_two = split_heads(key_two, row_count)
    value_heads_two = split_heads(value_two, row_count)
    mixed_two, lse_two = attend(query_heads_two, key_heads_two, value_heads_two, 0.0, cross_allowed)
    mixed_two = mixed_two.reshape(row_count * block_len, model_width)
    hidden_two = hidden_one + matmul(mixed_two, cross_full[4])
    norm_three, factor_three = rms_forward(hidden_two, ffn_full[0])
    gate_value = matmul(norm_three, ffn_full[1])
    up_value = matmul(norm_three, ffn_full[2])
    activation, geglu_back = jax.vjp(geglu, gate_value, up_value)
    hidden_act = activation.astype(jnp.bfloat16)
    result = hidden_two + matmul(hidden_act, ffn_full[3])
    output = result.astype(jnp.bfloat16).reshape(row_count, block_len, model_width)
    self_back = self_full
    cross_back = cross_full
    ffn_back = ffn_full
    grad_out = cotangent.reshape(row_count * block_len, model_width).astype(jnp.float32)
    low_out = grad_out.astype(jnp.bfloat16)
    grad_down = contract_rows(hidden_act, low_out)
    grad_hidden = times_transposed(low_out, ffn_back[3])
    grad_gate, grad_up = geglu_back(grad_hidden)
    low_gate = grad_gate.astype(jnp.bfloat16)
    low_up = grad_up.astype(jnp.bfloat16)
    low_in = jnp.concatenate([low_gate, low_up], axis=1)
    summed_in = scatter_rows(contract_rows(norm_three, low_in).astype(jnp.bfloat16))
    summed_down = scatter_rows(grad_down.astype(jnp.bfloat16))
    grad_norm_three = times_transposed(low_in, packed_in)
    grad_residual_three, grad_gain_three = rms_backward(
        hidden_two, factor_three, ffn_back[0], grad_norm_three
    )
    grad_two = grad_out + grad_residual_three
    low_two = grad_two.astype(jnp.bfloat16)
    grad_cross_out = contract_rows(mixed_two, low_two)
    grad_mixed_two = times_transposed(low_two, cross_back[4]).astype(jnp.bfloat16)
    unused_scores, grad_query_two, grad_key_part_two, grad_value_part_two = attend_back(
        query_heads_two,
        key_heads_two,
        value_heads_two,
        0.0,
        cross_allowed,
        lse_two,
        split_heads(grad_mixed_two, row_count),
    )
    pair_two = jnp.concatenate(
        [
            grad_key_part_two.reshape(row_count, enc_len, model_width),
            grad_value_part_two.reshape(row_count, enc_len, model_width),
        ],
        axis=2,
    ).astype(jnp.bfloat16)
    low_pair_two = scatter_to_owner(pair_two, row_count, enc_block).reshape(
        row_count * enc_block, 2 * model_width
    )
    grad_cross_pair = contract_rows(enc_own, low_pair_two)
    grad_encoder = times_transposed(
        low_pair_two, packed_cross[:, model_width : 3 * model_width]
    ).reshape(row_count, enc_block, model_width)
    low_query_two = grad_query_two.reshape(row_count * block_len, model_width)
    grad_cross_query = contract_rows(norm_two, low_query_two)
    grad_norm_two = times_transposed(low_query_two, cross_back[1])
    summed_cross = scatter_rows(
        jnp.concatenate([grad_cross_query, grad_cross_pair, grad_cross_out], axis=1).astype(
            jnp.bfloat16
        )
    )
    grad_residual_two, grad_gain_two = rms_backward(
        hidden_one, factor_two, cross_back[0], grad_norm_two
    )
    grad_one = grad_two + grad_residual_two
    low_one = grad_one.astype(jnp.bfloat16)
    grad_self_out = contract_rows(mixed_one, low_one)
    grad_mixed_one = times_transposed(low_one, self_back[4]).astype(jnp.bfloat16)
    grad_scores_one, grad_query_one, grad_key_part_one, grad_value_part_one = attend_back(
        query_heads_one,
        key_heads_one,
        value_heads_one,
        position_bias[None],
        self_allowed,
        lse_one,
        split_heads(grad_mixed_one, row_count),
    )
    grad_table = jnp.einsum(
        "qbk,rhqk->bh", onehot.astype(jnp.float32), grad_scores_one, precision=highest
    )
    pair_one = jnp.concatenate(
        [
            grad_key_part_one.reshape(row_count, full_len, model_width),
            grad_value_part_one.reshape(row_count, full_len, model_width),
        ],
        axis=2,
    ).astype(jnp.bfloat16)
    low_pair_one = scatter_to_owner(pair_one, row_count, block_len).reshape(
        row_count * block_len, 2 * model_width
    )
    low_query_one = grad_query_one.reshape(row_count * block_len, model_width)
    low_qkv_one = jnp.concatenate([low_query_one, low_pair_one], axis=1)
    grad_self_qkv = contract_rows(norm_one, low_qkv_one)
    grad_norm_one = times_transposed(low_qkv_one, packed_self[:, : 3 * model_width])
    grad_residual_one, grad_gain_one = rms_backward(
        inputs_flat, factor_one, self_back[0], grad_norm_one
    )
    grad_tokens = (grad_one + grad_residual_one).reshape(row_count, block_len, model_width)
    summed_self = scatter_rows(
        jnp.concatenate([grad_self_qkv, grad_self_out], axis=1).astype(jnp.bfloat16)
    )
    table_items = grad_table.size
    small_parts = jnp.concatenate(
        [grad_table.reshape(-1), grad_gain_one, grad_gain_two, grad_gain_three]
    )
    small_sum = sum_everywhere(small_parts.reshape(-1, 128)).reshape(-1)
    table_grad = small_sum[:table_items].reshape(grad_table.shape)
    own_index = lax.axis_index("fsdp") * seq_count + seq_index

    def flat_columns(summed, start, width):
        return summed[:, start : start + width].reshape(-1).astype(jnp.float32)

    def gain_grad(index):
        start = table_items + index * model_width + own_index * own_rows
        return lax.dynamic_slice_in_dim(small_sum, start, own_rows, 0)

    return (
        output,
        grad_tokens,
        grad_encoder,
        gain_grad(0),
        *[flat_columns(summed_self, index * model_width, model_width) for index in range(4)],
        table_grad,
        gain_grad(1),
        *[flat_columns(summed_cross, index * model_width, model_width) for index in range(4)],
        gain_grad(2),
        flat_columns(summed_in, 0, hidden_width),
        flat_columns(summed_in, hidden_width, hidden_width),
        summed_down.reshape(-1).astype(jnp.float32),
    )


def solution(mesh):
    in_specs = (
        P("fsdp", "seq", None),
        P("fsdp", None, None),
        P("fsdp", None),
        P("fsdp", None),
        P(),
        P(("fsdp", "seq")),
        P(("fsdp", "seq")),
        P(("fsdp", "seq")),
        P(("fsdp", "seq")),
        P(("fsdp", "seq")),
        P(),
        P(("fsdp", "seq")),
        P(("fsdp", "seq")),
        P(("fsdp", "seq")),
        P(("fsdp", "seq")),
        P(("fsdp", "seq")),
        P(("fsdp", "seq")),
        P(("fsdp", "seq")),
        P(("fsdp", "seq")),
        P(("fsdp", "seq")),
        P("fsdp", "seq", None),
    )
    out_specs = (
        P("fsdp", "seq", None),
        P("fsdp", "seq", None),
        P("fsdp", "seq", None),
        P(("fsdp", "seq")),
        P(("fsdp", "seq")),
        P(("fsdp", "seq")),
        P(("fsdp", "seq")),
        P(("fsdp", "seq")),
        P(),
        P(("fsdp", "seq")),
        P(("fsdp", "seq")),
        P(("fsdp", "seq")),
        P(("fsdp", "seq")),
        P(("fsdp", "seq")),
        P(("fsdp", "seq")),
        P(("fsdp", "seq")),
        P(("fsdp", "seq")),
        P(("fsdp", "seq")),
    )
    return jax.shard_map(
        per_device, mesh=mesh, in_specs=in_specs, out_specs=out_specs, check_vma=False
    )
```

profile of v0, /device:TPU:0, one launch (start us, length us, event | category | flops | bytes accessed | tf_op | source)
XLA Modules:
  0.0 729.4 jit_solution(9494032237790957650)
XLA Ops:
  15.5 63.9 %all-gather.6.cloned.1.call-done = bf16[768,3200]{1,0:T(8,128)(2,1)} async-done(((bf16[24,3200]{1,0:T(8,128)(2,1)}), bf16[768,3200]{1,0:T(8,128)(2,1)}) %all-gather.6.cloned.1.call-update) | async-done | bytes 4915216 | tf_op jit(solution)/shard_map/all_gather | solution.py:43
  81.5 2.9 convolution_convert_fusion.2
  87.6 3.9 fusion.1
  91.5 5.5 copy.111
  97.3 43.5 %all-gather.10.cloned.1.call-done = bf16[2048,768]{1,0:T(8,128)(2,1)} async-done(((bf16[64,768]{1,0:T(8,128)(2,1)}), bf16[2048,768]{1,0:T(8,128)(2,1)}) %all-gather.10.cloned.1.call-update) | async-done | bytes 3145744 | tf_op jit(solution)/shard_map/all_gather | solution.py:43
  140.7 4.0 fusion.75
  145.0 16.4 %all-gather.12.cloned.1.call-done = bf16[512,1536]{1,0:T(8,128)(2,1)} async-done(((bf16[128,1536]{1,0:T(8,128)(2,1)}), bf16[512,1536]{1,0:T(8,128)(2,1)}) %all-gather.12.cloned.1.call-update) | async-done | bytes 1572880 | tf_op jit(solution)/shard_map/all_gather | solution.py:210
  163.5 2.9 fusion.97
  170.6 82.5 %all-gather.8.cloned.1.call-done = bf16[768,7168]{1,0:T(8,128)(2,1)} async-done(((bf16[24,7168]{1,0:T(8,128)(2,1)}), bf16[768,7168]{1,0:T(8,128)(2,1)}) %all-gather.8.cloned.1.call-update) | async-done | bytes 11010064 | tf_op jit(solution)/shard_map/all_gather | solution.py:43
  266.0 2.8 multiply_reduce_fusion.2
  268.8 2.8 convolution_convert_fusion.4
  274.1 3.6 multiply_reduce_fusion.1
  293.7 6.6 collective-permute-done.5
  305.2 2.8 multiply_reduce_fusion.3
  323.5 10.8 %collective-permute-done = bf16[1,128,1536]{1,2,0:T(8,128)(2,1)S(1)} collective-permute-done((bf16[1,128,1536]{1,2,0:T(8,128)(2,1)S(1)}, bf16[1,128,1536]{1,2,0:T(8,128)(2,1)S(1)}, u32[]{:S(2)}, u32[]{:S(2)}) %collective-permute-start) | collective-permute-done | bytes 393248 | tf_op jit(solution)/shard_map/ppermute | solution.py:58
  335.1 5.9 collective-permute-done.2
  346.6 4.5 convolution_convert_fusion
  352.9 3.5 copy.115
  356.5 6.5 fusion.29
  363.7 5.0 fusion.61
  379.1 3.4 fusion.22
  393.9 94.4 %reduce-scatter.7.cloned.1.call-done = bf16[24,3072]{1,0:T(8,128)(2,1)} async-done(((bf16[768,3072]{1,0:T(8,128)(2,1)}), bf16[24,3072]{1,0:T(8,128)(2,1)}) %reduce-scatter.7.cloned.1.call-update) | async-done | bytes 147472 | tf_op jit(solution)/shard_map/reduce_scatter | solution.py:47
  491.6 109.0 %reduce-scatter.5.cloned.1.call-done = bf16[24,3072]{1,0:T(8,128)(2,1)} async-done(((bf16[768,3072]{1,0:T(8,128)(2,1)}), bf16[24,3072]{1,0:T(8,128)(2,1)}) %reduce-scatter.5.cloned.1.call-update) | async-done | bytes 147472 | tf_op jit(solution)/shard_map/reduce_scatter | solution.py:47
  604.1 115.9 %reduce-scatter.9.cloned.1.call-done = bf16[24,4096]{1,0:T(8,128)(2,1)} async-done(((bf16[768,4096]{1,0:T(8,128)(2,1)}), bf16[24,4096]{1,0:T(8,128)(2,1)}) %reduce-scatter.9.cloned.1.call-update) | async-done | bytes 196624 | tf_op jit(solution)/shard_map/reduce_scatter | solution.py:47
  (340 shorter events, 110.6 us)
Async XLA Ops:
  7.2 247.7 %copy-start = (bf16[1,512,768]{2,1,0:T(8,128)(2,1)S(1)}, bf16[1,512,768]{2,1,0:T(8,128)(2,1)}, u32[]{:S(2)}) copy-start(bf16[1,512,768]{2,1,0:T(8,128)(2,1)} %param.22) | copy-start | bytes 2359300
  7.2 72.2 %all-gather.6.cloned.1.call-start = ((), (), s32[]{:S(2)}) async-start(), calls=%async_computation.4 | async-start | bytes 5068800 | tf_op jit(solution)/shard_map/all_gather | solution.py:43
  12.2 128.6 %all-gather.10.cloned.1.call-start = ((), (), s32[]{:S(2)}) async-start(), calls=%async_computation.6 | async-start | bytes 3244032 | tf_op jit(solution)/shard_map/all_gather | solution.py:43
  13.9 147.5 %all-gather.12.cloned.1.call-start = ((), (), s32[]{:S(2)}) async-start(), calls=%async_computation.11 | async-start | bytes 1966080 | tf_op jit(solution)/shard_map/all_gather | solution.py:210
  81.5 171.6 %copy-start.59 = (f32[768]{0:T(1024)}, f32[768]{0:T(1024)S(1)}, u32[]{:S(2)}) copy-start(f32[768]{0:T(1024)S(1)} %get-tuple-element.91) | copy-start | bytes 9220
  85.2 167.8 %all-gather.8.cloned.1.call-start = ((), (), s32[]{:S(2)}) async-start(), calls=%async_computation.5 | async-start | bytes 11354112 | tf_op jit(solution)/shard_map/all_gather | solution.py:43
  86.5 305.7 %reduce-scatter.11.cloned.1.call-start = ((), (), s32[]{:S(2)}) async-start(), calls=%async_computation.10 | async-start | bytes 3244032 | tf_op jit(solution)/shard_map/reduce_scatter | solution.py:47
  97.3 164.5 %copy-start.24 = (pred[128,512]{1,0:T(8,128)(4,1)}, pred[128,512]{1,0:T(8,128)(4,1)S(1)}, u32[]{:S(2)}) copy-start(pred[128,512]{1,0:T(8,128)(4,1)S(1)} %get-tuple-element.131) | copy-start | bytes 196612
  170.0 114.8 %copy-start.16 = (f32[128,768]{1,0:T(8,128)}, f32[128,768]{1,0:T(8,128)S(1)}, u32[]{:S(2)}) copy-start(f32[128,768]{1,0:T(8,128)S(1)} %get-tuple-element.136) | copy-start | bytes 1179652
  271.7 216.6 %reduce-scatter.7.cloned.1.call-start = ((), (), s32[]{:S(2)}) async-start(), calls=%async_computation.8 | async-start | bytes 4866048 | tf_op jit(solution)/shard_map/reduce_scatter | solution.py:47
  281.1 10.9 %collective-permute-start.3 = (bf16[1,128,1536]{1,2,0:T(8,128)(2,1)}, bf16[1,128,1536]{1,2,0:T(8,128)(2,1)}, u32[]{:S(2)}, u32[]{:S(2)}) collective-permute-start(bf16[1,128,1536]{1,2,0:T(8,128)(2,1)} %get-tuple-element.104), channel_id=1, source_target_pairs={{0,1},{1,2},{2,3},{3,0},{4,5},{5,6},{6,7},{7,4},{8,9},{9,10},{10,1... | collective-permute-start | bytes 1179656 | tf_op jit(solution)/shard_map/ppermute | solution.py:58
  281.4 12.3 %collective-permute-start.4 = (bf16[1,128,1536]{1,2,0:T(8,128)(2,1)}, bf16[1,128,1536]{1,2,0:T(8,128)(2,1)}, u32[]{:S(2)}, u32[]{:S(2)}) collective-permute-start(bf16[1,128,1536]{1,2,0:T(8,128)(2,1)} %get-tuple-element.105), channel_id=1, source_target_pairs={{0,2},{1,3},{2,0},{3,1},{4,6},{5,7},{6,4},{7,5},{8,10},{9,11},{10,... | collective-permute-start | bytes 1179656 | tf_op jit(solution)/shard_map/ppermute | solution.py:58
  282.9 17.4 %collective-permute-start.5 = (bf16[1,128,1536]{1,2,0:T(8,128)(2,1)}, bf16[1,128,1536]{1,2,0:T(8,128)(2,1)}, u32[]{:S(2)}, u32[]{:S(2)}) collective-permute-start(bf16[1,128,1536]{1,2,0:T(8,128)(2,1)} %get-tuple-element.106), channel_id=1, source_target_pairs={{0,3},{1,0},{2,1},{3,2},{4,7},{5,4},{6,5},{7,6},{8,11},{9,8},{10,9... | collective-permute-start | bytes 1179656 | tf_op jit(solution)/shard_map/ppermute | solution.py:58
  305.2 295.5 %reduce-scatter.5.cloned.1.call-start = ((), (), s32[]{:S(2)}) async-start(), calls=%async_computation.7 | async-start | bytes 4866048 | tf_op jit(solution)/shard_map/reduce_scatter | solution.py:47
  319.6 14.6 %collective-permute-start = (bf16[1,128,1536]{1,2,0:T(8,128)(2,1)S(1)}, bf16[1,128,1536]{1,2,0:T(8,128)(2,1)S(1)}, u32[]{:S(2)}, u32[]{:S(2)}) collective-permute-start(bf16[1,128,1536]{1,2,0:T(8,128)(2,1)S(1)} %get-tuple-element.107), channel_id=1, source_target_pairs={{0,1},{1,2},{2,3},{3,0},{4,5},{5,6},{6,7},{7,4},{8,9},{9,10},{10,1... | collective-permute-start | bytes 1179656 | tf_op jit(solution)/shard_map/ppermute | solution.py:58
  320.6 14.5 %collective-permute-start.1 = (bf16[1,128,1536]{1,2,0:T(8,128)(2,1)S(1)}, bf16[1,128,1536]{1,2,0:T(8,128)(2,1)S(1)}, u32[]{:S(2)}, u32[]{:S(2)}) collective-permute-start(bf16[1,128,1536]{1,2,0:T(8,128)(2,1)S(1)} %get-tuple-element.108), channel_id=1, source_target_pairs={{0,2},{1,3},{2,0},{3,1},{4,6},{5,7},{6,4},{7,5},{8,10},{9,11},{10,... | collective-permute-start | bytes 1179656 | tf_op jit(solution)/shard_map/ppermute | solution.py:58
  322.1 18.9 %collective-permute-start.2 = (bf16[1,128,1536]{1,2,0:T(8,128)(2,1)S(1)}, bf16[1,128,1536]{1,2,0:T(8,128)(2,1)S(1)}, u32[]{:S(2)}, u32[]{:S(2)}) collective-permute-start(bf16[1,128,1536]{1,2,0:T(8,128)(2,1)S(1)} %get-tuple-element.109), channel_id=1, source_target_pairs={{0,3},{1,0},{2,1},{3,2},{4,7},{5,4},{6,5},{7,6},{8,11},{9,8},{10,9... | collective-permute-start | bytes 1179656 | tf_op jit(solution)/shard_map/ppermute | solution.py:58
  345.3 374.7 %reduce-scatter.9.cloned.1.call-start = ((), (), s32[]{:S(2)}) async-start(), calls=%async_computation.9 | async-start | bytes 6488064 | tf_op jit(solution)/shard_map/reduce_scatter | solution.py:47
  369.9 3.0 collective-permute-start.6
  373.8 3.8 collective-permute-start.7
  377.6 5.0 collective-permute-start.8
  379.1 343.3 %copy-start.1 = (bf16[1,512,768]{2,1,0:T(8,128)(2,1)S(1)}, bf16[1,512,768]{2,1,0:T(8,128)(2,1)}, u32[]{:S(2)}) copy-start(bf16[1,512,768]{2,1,0:T(8,128)(2,1)} %param.22) | copy-start | bytes 2359300
  382.5 3.7 collective-permute-start.9
  386.2 4.6 collective-permute-start.10
  (90 other events, 846.4 us)
Sparse Core Ops, SparseCore 0:
  12.3 67.0 all-gather.5
  82.8 57.8 all-gather.9
  142.9 18.4 all-gather.11
  164.2 88.8 all-gather.7
  271.8 105.0 reduce-scatter.10
  382.2 105.9 reduce-scatter.6
  494.6 106.0 reduce-scatter.4
  606.3 113.5 reduce-scatter.8
where the time goes:
time: 735 us; the launch traced here: 729 us
  waiting for transfers between devices  558 us (76%)
  matrix products  74.8 us (10%)
  local copies, waits for them, and re-layouts  42.6 us (6%)
  other arithmetic  24.3 us (3%)
  between operations  15.9 us (2%)
  starting transfers between devices  13.7 us (2%)
    reduce_scatter x4, waiting for transfers between devices, scatter_rows(): lax.psum_scatter(partial, ('fsdp', 'seq'), scatter_dimension=0, tiled=True)  319 us
    all_gather x3, waiting for transfers between devices, gather_rows(): return lax.all_gather(packed, ('fsdp', 'seq'), axis=0, tiled=True)  190 us
    ppermute x6, waiting for transfers between devices, scatter_to_owner(): total = total + lax.ppermute(piece, 'seq', pairs).astype(jnp.float32)  27 us
    dot_general x7, matrix products, times_transposed(): lax.dot_general(first_op, second_op, (((1,), (1,)), ((), ())), preferred_...  22.6 us
    all_gather x1, waiting for transfers between devices, per_device(): lax.all_gather(qkv_one[:, model_width:].reshape(row_count, block_len, 2 *...  16.4 us
  transfers between devices with their start and end apart: 19, of which 17 were waited for; matrix products, arithmetic and copies ran while one was open for 15% of the time, Pallas kernels for 0%

commit v1 on v0

--- a/solution.py
+++ b/solution.py
@@ -1,3 +1,4 @@
+import functools
 import jax
 import jax.numpy as jnp
 from jax import lax
@@ -8,6 +9,35 @@
 epsilon = 1e-06
 masked_value = -1e30
 highest = lax.Precision.HIGHEST
+
+
+def state_inputs(local_array, d_out):
+    new = list(local_array.shape[1:])
+    new[d_out] *= local_array.shape[0]
+    vec_out = jnp.moveaxis(local_array, 0, d_out).reshape(new)
+    return vec_out
+
+
+def _update_tasks(panel, bus_axis, dim_at):
+    sides = lax.axis_size(bus_axis)
+    slots = [(dd, (dd + 1) % sides) for dd in range(sides)]
+    xs_all = [(k0, i) for i, k0 in slots]
+    local_part, parts_out = ([], [])
+    for i0 in range(sides - 1):
+        if i0 % 2 == 0:
+            local_part.append(
+                lax.ppermute(local_part[-1] if local_part else panel, bus_axis, slots)
+            )
+        else:
+            parts_out.append(lax.ppermute(parts_out[-1] if parts_out else panel, bus_axis, xs_all))
+    y2 = jnp.stack([*local_part[::-1], panel, *parts_out])
+    piece_next = lax.axis_index(bus_axis) - len(local_part)
+    y2 = y2[(jnp.arange(sides) - piece_next) % sides]
+    f_next = state_inputs(y2, dim_at)
+    return f_next
+
+
+derive_joints = functools.partial(_update_tasks, bus_axis="seq", dim_at=1)
 
 
 def matmul(first_op, second_op):
@@ -207,11 +237,8 @@
     norm_one, factor_one = rms_forward(inputs_flat, self_full[0])
     qkv_one = matmul(norm_one, packed_self[:, : 3 * model_width]).astype(jnp.bfloat16)
     query_one = qkv_one[:, :model_width]
-    pair_all = lax.all_gather(
-        qkv_one[:, model_width:].reshape(row_count, block_len, 2 * model_width),
-        "seq",
-        axis=1,
-        tiled=True,
+    pair_all = derive_joints(
+        qkv_one[:, model_width:].reshape(row_count, block_len, 2 * model_width)
     )
     key_all = pair_all[:, :, :model_width]
     value_all = pair_all[:, :, model_width:]

time: 735 us -> 714 us (0.971)
  waiting for transfers between devices: 558 us -> 527 us
    all_gather x1 -> x0, waiting for transfers between devices: 16.4 us -> none  [per_device(): lax.all_gather(qkv_one[:, model_width:].reshape(row_count, block_len, 2 *...]
    all_gather x3, waiting for transfers between devices: 190 us -> 175 us  [gather_rows(): return lax.all_gather(packed, ('fsdp', 'seq'), axis=0, tiled=True)]
  transfers between devices with their start and end apart: 19 -> 21, of which waited for: 17 -> 17; matrix products, arithmetic and copies ran while one was open for 15% -> 16% of each run, Pallas kernels for 0% -> 0%
where the time goes in v1:
time: 714 us; the launch traced here: 708 us
  waiting for transfers between devices  527 us (74%)
  matrix products  74.7 us (10%)
  local copies, waits for them, and re-layouts  49.8 us (7%)
  other arithmetic  24.9 us (3%)
  starting transfers between devices  15.8 us (2%)
  between operations  15.7 us (2%)
    reduce_scatter x4, waiting for transfers between devices, scatter_rows(): lax.psum_scatter(partial, ('fsdp', 'seq'), scatter_dimension=0, tiled=True)  319 us
    all_gather x3, waiting for transfers between devices, gather_rows(): return lax.all_gather(packed, ('fsdp', 'seq'), axis=0, tiled=True)  175 us
    ppermute x6, waiting for transfers between devices, scatter_to_owner(): total = total + lax.ppermute(piece, 'seq', pairs).astype(jnp.float32)  27 us
    dot_general x7, matrix products, times_transposed(): lax.dot_general(first_op, second_op, (((1,), (1,)), ((), ())), preferred_...  22.7 us
  transfers between devices with their start and end apart: 21, of which 17 were waited for; matrix products, arithmetic and copies ran while one was open for 16% of the time, Pallas kernels for 0%

profile of v1, /device:TPU:0, one launch (start us, length us, event | category | flops | bytes accessed | tf_op | source)
XLA Modules:
  0.0 707.8 jit_solution(18231951533675399978)
XLA Ops:
  21.2 3.9 fusion.1
  25.1 54.4 %all-gather.4.cloned.1.call-done = bf16[768,3200]{1,0:T(8,128)(2,1)} async-done(((bf16[24,3200]{1,0:T(8,128)(2,1)}), bf16[768,3200]{1,0:T(8,128)(2,1)}) %all-gather.4.cloned.1.call-update) | async-done | bytes 4915216 | tf_op jit(solution)/shard_map/all_gather | solution.py:73
  81.6 2.7 convolution_convert_fusion.2
  85.5 5.0 copy.109
  93.0 47.8 %all-gather.8.cloned.1.call-done = bf16[2048,768]{1,0:T(8,128)(2,1)} async-done(((bf16[64,768]{1,0:T(8,128)(2,1)}), bf16[2048,768]{1,0:T(8,128)(2,1)}) %all-gather.8.cloned.1.call-update) | async-done | bytes 3145744 | tf_op jit(solution)/shard_map/all_gather | solution.py:73
  140.8 4.0 fusion.75
  151.8 3.1 fusion.99
  159.1 72.6 %all-gather.6.cloned.1.call-done = bf16[768,7168]{1,0:T(8,128)(2,1)} async-done(((bf16[24,7168]{1,0:T(8,128)(2,1)}), bf16[768,7168]{1,0:T(8,128)(2,1)}) %all-gather.6.cloned.1.call-update) | async-done | bytes 11010064 | tf_op jit(solution)/shard_map/all_gather | solution.py:73
  244.6 3.0 multiply_reduce_fusion.2
  247.6 2.7 convolution_convert_fusion.4
  252.7 3.6 multiply_reduce_fusion.1
  272.3 6.6 collective-permute-done.8
  283.8 2.8 multiply_reduce_fusion.3
  302.1 10.8 %collective-permute-done.3 = bf16[1,128,1536]{1,2,0:T(8,128)(2,1)S(1)} collective-permute-done((bf16[1,128,1536]{1,2,0:T(8,128)(2,1)S(1)}, bf16[1,128,1536]{1,2,0:T(8,128)(2,1)S(1)}, u32[]{:S(2)}, u32[]{:S(2)}) %collective-permute-start.3) | collective-permute-done | bytes 393248 | tf_op jit(solution)/shard_map/ppermute | solution.py:88
  313.7 5.9 collective-permute-done.5
  321.0 2.8 pad_maximum_fusion
  325.2 4.4 convolution_convert_fusion
  331.5 3.5 copy.113
  335.0 6.5 fusion.29
  342.3 5.0 fusion.61
  357.7 3.4 fusion.22
  372.5 94.4 %reduce-scatter.7.cloned.1.call-done = bf16[24,3072]{1,0:T(8,128)(2,1)} async-done(((bf16[768,3072]{1,0:T(8,128)(2,1)}), bf16[24,3072]{1,0:T(8,128)(2,1)}) %reduce-scatter.7.cloned.1.call-update) | async-done | bytes 147472 | tf_op jit(solution)/shard_map/reduce_scatter | solution.py:77
  470.2 109.0 %reduce-scatter.5.cloned.1.call-done = bf16[24,3072]{1,0:T(8,128)(2,1)} async-done(((bf16[768,3072]{1,0:T(8,128)(2,1)}), bf16[24,3072]{1,0:T(8,128)(2,1)}) %reduce-scatter.5.cloned.1.call-update) | async-done | bytes 147472 | tf_op jit(solution)/shard_map/reduce_scatter | solution.py:77
  582.6 115.7 %reduce-scatter.9.cloned.1.call-done = bf16[24,4096]{1,0:T(8,128)(2,1)} async-done(((bf16[768,4096]{1,0:T(8,128)(2,1)}), bf16[24,4096]{1,0:T(8,128)(2,1)}) %reduce-scatter.9.cloned.1.call-update) | async-done | bytes 196624 | tf_op jit(solution)/shard_map/reduce_scatter | solution.py:77
  (337 shorter events, 118.5 us)
Async XLA Ops:
  7.2 226.3 %copy-start = (bf16[1,512,768]{2,1,0:T(8,128)(2,1)S(1)}, bf16[1,512,768]{2,1,0:T(8,128)(2,1)}, u32[]{:S(2)}) copy-start(bf16[1,512,768]{2,1,0:T(8,128)(2,1)} %param.22) | copy-start | bytes 2359300
  7.2 72.2 %all-gather.4.cloned.1.call-start = ((), (), s32[]{:S(2)}) async-start(), calls=%async_computation.4 | async-start | bytes 5068800 | tf_op jit(solution)/shard_map/all_gather | solution.py:73
  12.2 128.6 %all-gather.8.cloned.1.call-start = ((), (), s32[]{:S(2)}) async-start(), calls=%async_computation.6 | async-start | bytes 3244032 | tf_op jit(solution)/shard_map/all_gather | solution.py:73
  14.0 217.7 %all-gather.6.cloned.1.call-start = ((), (), s32[]{:S(2)}) async-start(), calls=%async_computation.5 | async-start | bytes 11354112 | tf_op jit(solution)/shard_map/all_gather | solution.py:73
  20.1 350.7 %reduce-scatter.11.cloned.1.call-start = ((), (), s32[]{:S(2)}) async-start(), calls=%async_computation.10 | async-start | bytes 3244032 | tf_op jit(solution)/shard_map/reduce_scatter | solution.py:77
  81.6 150.1 %copy-start.58 = (f32[768]{0:T(1024)}, f32[768]{0:T(1024)S(1)}, u32[]{:S(2)}) copy-start(f32[768]{0:T(1024)S(1)} %get-tuple-element.91) | copy-start | bytes 9220
  85.1 7.4 %collective-permute-start = (bf16[1,128,1536]{2,1,0:T(8,128)(2,1)}, bf16[1,128,1536]{2,1,0:T(8,128)(2,1)S(1)}, u32[]{:S(2)}, u32[]{:S(2)}) collective-permute-start(bf16[1,128,1536]{2,1,0:T(8,128)(2,1)} %get-tuple-element.113), channel_id=1, source_target_pairs={{0,1},{1,2},{2,3},{3,0},{4,5},{5,6},{6,7},{7,4},{8,9},{9,10},{10,1... | collective-permute-start | bytes 1179656 | tf_op jit(solution)/shard_map/ppermute | solution.py:29
  90.7 55.0 %collective-permute-start.2 = (bf16[1,128,1536]{2,1,0:T(8,128)(2,1)}, bf16[1,128,1536]{2,1,0:T(8,128)(2,1)S(1)}, u32[]{:S(2)}, u32[]{:S(2)}) collective-permute-start(bf16[1,128,1536]{2,1,0:T(8,128)(2,1)} %get-tuple-element.113), channel_id=1, source_target_pairs={{1,0},{2,1},{3,2},{0,3},{5,4},{6,5},{7,6},{4,7},{9,8},{10,9},{11,1... | collective-permute-start | bytes 1179656 | tf_op jit(solution)/shard_map/ppermute | solution.py:32
  92.5 53.1 %collective-permute-start.1 = (bf16[1,128,1536]{2,1,0:T(8,128)(2,1)S(1)}, bf16[1,128,1536]{2,1,0:T(8,128)(2,1)}, u32[]{:S(2)}, u32[]{:S(2)}) collective-permute-start(bf16[1,128,1536]{2,1,0:T(8,128)(2,1)S(1)} %collective-permute-done), channel_id=1, source_target_pairs={{0,1},{1,2},{2,3},{3,0},{4,5},{5,6},{6,7},{7,4},{8,9},{9,10},{10,1... | collective-permute-start | bytes 1179656 | tf_op jit(solution)/shard_map/ppermute | solution.py:29
  250.3 216.5 %reduce-scatter.7.cloned.1.call-start = ((), (), s32[]{:S(2)}) async-start(), calls=%async_computation.8 | async-start | bytes 4866048 | tf_op jit(solution)/shard_map/reduce_scatter | solution.py:77
  259.7 10.9 %collective-permute-start.6 = (bf16[1,128,1536]{1,2,0:T(8,128)(2,1)}, bf16[1,128,1536]{1,2,0:T(8,128)(2,1)}, u32[]{:S(2)}, u32[]{:S(2)}) collective-permute-start(bf16[1,128,1536]{1,2,0:T(8,128)(2,1)} %get-tuple-element.104), channel_id=1, source_target_pairs={{0,1},{1,2},{2,3},{3,0},{4,5},{5,6},{6,7},{7,4},{8,9},{9,10},{10,1... | collective-permute-start | bytes 1179656 | tf_op jit(solution)/shard_map/ppermute | solution.py:88
  260.0 12.3 %collective-permute-start.7 = (bf16[1,128,1536]{1,2,0:T(8,128)(2,1)}, bf16[1,128,1536]{1,2,0:T(8,128)(2,1)}, u32[]{:S(2)}, u32[]{:S(2)}) collective-permute-start(bf16[1,128,1536]{1,2,0:T(8,128)(2,1)} %get-tuple-element.105), channel_id=1, source_target_pairs={{0,2},{1,3},{2,0},{3,1},{4,6},{5,7},{6,4},{7,5},{8,10},{9,11},{10,... | collective-permute-start | bytes 1179656 | tf_op jit(solution)/shard_map/ppermute | solution.py:88
  261.5 17.4 %collective-permute-start.8 = (bf16[1,128,1536]{1,2,0:T(8,128)(2,1)}, bf16[1,128,1536]{1,2,0:T(8,128)(2,1)}, u32[]{:S(2)}, u32[]{:S(2)}) collective-permute-start(bf16[1,128,1536]{1,2,0:T(8,128)(2,1)} %get-tuple-element.106), channel_id=1, source_target_pairs={{0,3},{1,0},{2,1},{3,2},{4,7},{5,4},{6,5},{7,6},{8,11},{9,8},{10,9... | collective-permute-start | bytes 1179656 | tf_op jit(solution)/shard_map/ppermute | solution.py:88
  283.8 295.4 %reduce-scatter.5.cloned.1.call-start = ((), (), s32[]{:S(2)}) async-start(), calls=%async_computation.7 | async-start | bytes 4866048 | tf_op jit(solution)/shard_map/reduce_scatter | solution.py:77
  298.3 14.6 %collective-permute-start.3 = (bf16[1,128,1536]{1,2,0:T(8,128)(2,1)S(1)}, bf16[1,128,1536]{1,2,0:T(8,128)(2,1)S(1)}, u32[]{:S(2)}, u32[]{:S(2)}) collective-permute-start(bf16[1,128,1536]{1,2,0:T(8,128)(2,1)S(1)} %get-tuple-element.107), channel_id=1, source_target_pairs={{0,1},{1,2},{2,3},{3,0},{4,5},{5,6},{6,7},{7,4},{8,9},{9,10},{10,1... | collective-permute-start | bytes 1179656 | tf_op jit(solution)/shard_map/ppermute | solution.py:88
  299.2 14.5 %collective-permute-start.4 = (bf16[1,128,1536]{1,2,0:T(8,128)(2,1)S(1)}, bf16[1,128,1536]{1,2,0:T(8,128)(2,1)S(1)}, u32[]{:S(2)}, u32[]{:S(2)}) collective-permute-start(bf16[1,128,1536]{1,2,0:T(8,128)(2,1)S(1)} %get-tuple-element.108), channel_id=1, source_target_pairs={{0,2},{1,3},{2,0},{3,1},{4,6},{5,7},{6,4},{7,5},{8,10},{9,11},{10,... | collective-permute-start | bytes 1179656 | tf_op jit(solution)/shard_map/ppermute | solution.py:88
  300.7 18.9 %collective-permute-start.5 = (bf16[1,128,1536]{1,2,0:T(8,128)(2,1)S(1)}, bf16[1,128,1536]{1,2,0:T(8,128)(2,1)S(1)}, u32[]{:S(2)}, u32[]{:S(2)}) collective-permute-start(bf16[1,128,1536]{1,2,0:T(8,128)(2,1)S(1)} %get-tuple-element.109), channel_id=1, source_target_pairs={{0,3},{1,0},{2,1},{3,2},{4,7},{5,4},{6,5},{7,6},{8,11},{9,8},{10,9... | collective-permute-start | bytes 1179656 | tf_op jit(solution)/shard_map/ppermute | solution.py:88
  323.9 374.4 %reduce-scatter.9.cloned.1.call-start = ((), (), s32[]{:S(2)}) async-start(), calls=%async_computation.9 | async-start | bytes 6488064 | tf_op jit(solution)/shard_map/reduce_scatter | solution.py:77
  348.5 3.0 collective-permute-start.9
  352.4 3.8 collective-permute-start.10
  356.1 5.0 collective-permute-start.11
  357.7 343.0 %copy-start.1 = (bf16[1,512,768]{2,1,0:T(8,128)(2,1)S(1)}, bf16[1,512,768]{2,1,0:T(8,128)(2,1)}, u32[]{:S(2)}) copy-start(bf16[1,512,768]{2,1,0:T(8,128)(2,1)} %param.22) | copy-start | bytes 2359300
  361.1 3.7 collective-permute-start.12
  364.8 4.6 collective-permute-start.13
  (87 other events, 1283.8 us)
Sparse Core Ops, SparseCore 0:
  12.4 67.0 all-gather.3
  82.9 57.8 all-gather.7
  143.7 87.9 all-gather.5
  250.4 105.0 reduce-scatter.10
  360.8 105.9 reduce-scatter.6
  473.0 106.0 reduce-scatter.4
  584.8 113.4 reduce-scatter.8
